TPU v7x, 32 devices: a whole 2x2x4 slice. The times are simulated.
32 devices in a mesh: dp: 16 (over z, y, core), fsdp: 2 (over x).
Axes of the slice: x: 2, y: 2, z: 4, core: 2. Of those that a mesh axis runs over, the one named last changes fastest.
Arguments:
- acts: bfloat16 [4096, 2048], P(('dp', 'fsdp')), may hold values from -6 to 6
- grad_out: bfloat16 [4096, 2048], P(('dp', 'fsdp')), may hold values from -60 to 60
- weight: bfloat16 [2048, 2048], P('fsdp'), may hold values from -0.125 to 0.125
- basis: bfloat16 [2048, 512], P('fsdp'), may hold values from -3 to 3
- first_moment: float32 [512, 2048], P(('dp', 'fsdp')), may hold values from -4 to 4
- second_moment: float32 [512, 2048], P(('dp', 'fsdp')), may hold values from 0.0001 to 0.01
Outputs:
- grad_in: bfloat16 [4096, 2048], P(('dp', 'fsdp'))
- first_new: float32 [512, 2048], P(('dp', 'fsdp'))
- second_new: float32 [512, 2048], P(('dp', 'fsdp'))
- weight_update: bfloat16 [2048, 2048], P('fsdp')
All inputs are finite; a program needn't handle non-finite values.
Results may differ from a plain program's by a relative error of at most 0.0056.
Values may be sent and summed in bfloat16 or wider, within the bound.
A program may use at most 64 MiB of HBM per device.

v0:
```python
import math

import jax
import jax.numpy as jnp
from jax import lax
from jax.sharding import PartitionSpec as P

D_OUT = 2048
RANK = 512


first_bias = 1.0 - 0.9**10
second_bias = 1.0 - 0.999**10


def on_device(acts, grad_out, weight, basis, first_moment, second_moment):
    contract_last = (((1,), (1,)), ((), ()))
    grad_in = lax.dot_general(
        grad_out,
        lax.all_gather(weight, "fsdp", axis=0, tiled=True),
        contract_last,
        preferred_element_type=jnp.float32,
    ).astype(jnp.bfloat16)
    columns = acts
    coords = jnp.dot(
        columns,
        lax.all_gather(basis, "fsdp", axis=0, tiled=True),
        preferred_element_type=jnp.float32,
    ).astype(jnp.bfloat16)
    projected = lax.psum_scatter(
        lax.dot_general(
            coords, grad_out, (((0,), (0,)), ((), ())), preferred_element_type=jnp.float32
        ),
        ("dp", "fsdp"),
        scatter_dimension=0,
        tiled=True,
    )
    total = lax.psum(jnp.sum(projected * projected), ("dp", "fsdp"))
    limit = math.sqrt(RANK * D_OUT)
    factor = jnp.minimum(1.0, limit / (jnp.sqrt(total) + 1e-06))
    clipped = factor * projected
    first_new = 0.9 * first_moment + 0.1 * clipped
    second_new = 0.999 * second_moment + 0.001 * clipped * clipped
    direction = (first_new / first_bias / (jnp.sqrt(second_new / second_bias) + 1e-08)).astype(
        jnp.bfloat16
    )
    columns = basis
    update = jnp.dot(
        columns,
        lax.all_gather(direction, ("dp", "fsdp"), axis=0, tiled=True),
        preferred_element_type=jnp.float32,
    )
    weight_update = (0.25 * update).astype(jnp.bfloat16)
    return (grad_in, first_new, second_new, weight_update)


def solution(mesh):
    in_specs = (
        P(("dp", "fsdp"), None),
        P(("dp", "fsdp"), None),
        P("fsdp", None),
        P("fsdp", None),
        P(("dp", "fsdp"), None),
        P(("dp", "fsdp"), None),
    )
    out_specs = (
        P(("dp", "fsdp"), None),
        P(("dp", "fsdp"), None),
        P(("dp", "fsdp"), None),
        P("fsdp", None),
    )
    return jax.shard_map(
        on_device, mesh=mesh, in_specs=in_specs, out_specs=out_specs, check_vma=False
    )
```

profile of v0, /device:TPU:1, one launch (start us, length us, event | category | flops | bytes accessed | tf_op | source)
XLA Modules:
  0.0 374.0 jit_solution(9531298871754880160)
XLA Ops:
  7.2 0.0 copy-start
  7.2 0.0 all-gather.6.cloned.1.call-start
  7.2 0.7 all-gather.6.cloned.1.call-update
  7.9 0.0 reduce-scatter.2.cloned.1.call-start
  8.0 36.8 %all-gather.6.cloned.1.call-done = bf16[2048,512]{1,0:T(8,128)(2,1)} async-done(((bf16[1024,512]{1,0:T(8,128)(2,1)}), bf16[2048,512]{1,0:T(8,128)(2,1)}) %all-gather.6.cloned.1.call-update) | async-done | bytes 2097168 | tf_op jit(solution)/shard_map/all_gather | solution.py:27
  44.8 0.0 copy-done
  44.8 5.0 %fusion.1 = f32[512,2048]{1,0:T(8,128)} fusion(bf16[128,2048]{1,0:T(8,128)(2,1)S(1)} %copy-done, bf16[128,2048]{1,0:T(8,128)(2,1)} %param.6, bf16[2048,512]{1,0:T(8,128)(2,1)} %all-gather.6.cloned.1.call-done), kind=kOutput, calls=%fused_computation.4 | convolution fusion | flops 536936448 | bytes 7340032 | tf_op jit(solution)/shard_map/dot_general | solution.py:31
  49.7 0.0 copy-start.2
  49.7 0.0 copy-start.3
  49.8 0.0 reduce-scatter.2.cloned.1.call-update
  49.8 0.0 all-gather.4.cloned.1.call-start
  49.8 0.7 all-gather.4.cloned.1.call-update
  50.5 0.0 all-gather.8.cloned.1.call-start
  50.6 139.0 %reduce-scatter.2.cloned.1.call-done = f32[16,2048]{1,0:T(8,128)} async-done(((f32[512,2048]{1,0:T(8,128)}), f32[16,2048]{1,0:T(8,128)}) %reduce-scatter.2.cloned.1.call-update) | async-done | bytes 131088 | tf_op jit(solution)/shard_map/reduce_scatter | solution.py:30
  189.6 1.5 multiply_reduce_fusion
  191.1 39.9 %psum.7 = f32[]{:T(128)} all-reduce(f32[]{:T(128)} %multiply_reduce_fusion), channel_id=1, replica_groups=mesh['dp'=16,'fsdp'=2] {'dp','fsdp'}, use_global_device_ids=true, to_apply=%region_2.0 | all-reduce | flops 1 | bytes 8 | tf_op jit(solution)/shard_map/psum | solution.py:38
  231.7 0.0 copy-done.2
  231.7 0.0 copy-done.3
  231.8 1.7 divide_convert_fusion
  233.4 0.0 all-gather.8.cloned.1.call-update
  233.5 0.0 copy-start.1
  233.5 61.4 %all-gather.4.cloned.1.call-done = bf16[2048,2048]{1,0:T(8,128)(2,1)} async-done(((bf16[1024,2048]{1,0:T(8,128)(2,1)}), bf16[2048,2048]{1,0:T(8,128)(2,1)}) %all-gather.4.cloned.1.call-update) | async-done | bytes 8388624 | tf_op jit(solution)/shard_map/all_gather | solution.py:20
  294.8 7.1 %convolution_convert_fusion = bf16[128,2048]{1,0:T(8,128)(2,1)} fusion(bf16[128,2048]{1,0:T(8,128)(2,1)S(1)} %copy-done, bf16[2048,2048]{1,0:T(8,128)(2,1)} %all-gather.4.cloned.1.call-done), kind=kOutput, calls=%fused_computation.2 | convolution fusion | flops 1074003968 | bytes 9437184 | tf_op jit(solution)/shard_map/dot_general | solution.py:18
  301.9 53.2 %all-gather.8.cloned.1.call-done = bf16[512,2048]{1,0:T(8,128)(2,1)} async-done(((bf16[16,2048]{1,0:T(8,128)(2,1)}), bf16[512,2048]{1,0:T(8,128)(2,1)}) %all-gather.8.cloned.1.call-update) | async-done | bytes 2097168 | tf_op jit(solution)/shard_map/all_gather | solution.py:50
  355.1 0.0 copy-done.1
  355.1 5.9 %fusion = bf16[1024,2048]{0,1:T(8,128)(2,1)} fusion(bf16[512,2048]{1,0:T(8,128)(2,1)} %all-gather.8.cloned.1.call-done, bf16[1024,512]{1,0:T(8,128)(2,1)S(1)} %copy-done.1), kind=kOutput, calls=%fused_computation.1 | convolution fusion | flops 2151677952 | bytes 7340032 | tf_op jit(solution)/shard_map/dot_general | solution.py:48
  361.0 6.4 %copy.10 = bf16[1024,2048]{1,0:T(8,128)(2,1)} copy(bf16[1024,2048]{0,1:T(8,128)(2,1)} %fusion) | data formatting | bytes 8388608
Async XLA Ops:
  7.2 37.6 %copy-start = (bf16[128,2048]{1,0:T(8,128)(2,1)S(1)}, bf16[128,2048]{1,0:T(8,128)(2,1)}, u32[]{:S(2)}) copy-start(bf16[128,2048]{1,0:T(8,128)(2,1)} %param.7) | copy-start | bytes 1572868
  7.2 37.6 %all-gather.6.cloned.1.call-start = ((), (), s32[]{:S(2)}) async-start(), calls=%async_computation.2 | async-start | bytes 3145728 | tf_op jit(solution)/shard_map/all_gather | solution.py:27
  7.9 181.7 %reduce-scatter.2.cloned.1.call-start = ((), (), s32[]{:S(2)}) async-start(), calls=%async_computation.3 | async-start | bytes 4325376 | tf_op jit(solution)/shard_map/reduce_scatter | solution.py:30
  49.7 182.0 %copy-start.2 = (f32[16,2048]{1,0:T(8,128)S(1)}, f32[16,2048]{1,0:T(8,128)}, u32[]{:S(2)}) copy-start(f32[16,2048]{1,0:T(8,128)} %param.11) | copy-start | bytes 393220
  49.7 182.0 %copy-start.3 = (f32[16,2048]{1,0:T(8,128)S(1)}, f32[16,2048]{1,0:T(8,128)}, u32[]{:S(2)}) copy-start(f32[16,2048]{1,0:T(8,128)} %param.10) | copy-start | bytes 393220
  49.8 245.0 %all-gather.4.cloned.1.call-start = ((), (), s32[]{:S(2)}) async-start(), calls=%async_computation.1 | async-start | bytes 12582912 | tf_op jit(solution)/shard_map/all_gather | solution.py:20
  50.5 304.6 %all-gather.8.cloned.1.call-start = ((), (), s32[]{:S(2)}) async-start(), calls=%async_computation.4 | async-start | bytes 2162688 | tf_op jit(solution)/shard_map/all_gather | solution.py:50
  233.5 121.6 %copy-start.1 = (bf16[1024,512]{1,0:T(8,128)(2,1)S(1)}, bf16[1024,512]{1,0:T(8,128)(2,1)}, u32[]{:S(2)}) copy-start(bf16[1024,512]{1,0:T(8,128)(2,1)} %param.9) | copy-start | bytes 3145732
Sparse Core Ops, SparseCore 0:
  9.6 35.1 all-gather.5
  49.9 139.6 reduce-scatter.1
  191.1 103.6 all-gather.3
  298.2 56.8 all-gather.7
where the time goes:
time: 375 us; the launch traced here: 374 us
  waiting for transfers between devices  292 us (78%)
  blocking collectives  39.9 us (11%)
  matrix products  17.9 us (5%)
  between operations  14.5 us (4%)
  local copies, waits for them, and re-layouts  6.45 us (2%)
    reduce_scatter x1, waiting for transfers between devices, on_device(): lax.psum_scatter(lax.dot_general(coords, grad_out, (((0,), (0,)), ((), ()...  139 us
    all_gather x1, waiting for transfers between devices, on_device(): lax.all_gather(weight, 'fsdp', axis=0, tiled=True)  61.4 us
    all_gather x1, waiting for transfers between devices, on_device(): lax.all_gather(direction, ('dp', 'fsdp'), axis=0, tiled=True)  53.2 us
    psum x1, blocking collectives, on_device(): total = lax.psum(jnp.sum(projected * projected), ('dp', 'fsdp'))  39.9 us
    all_gather x1, waiting for transfers between devices, on_device(): lax.all_gather(basis, 'fsdp', axis=0, tiled=True)  36.8 us
  transfers between devices with their start and end apart: 4, of which 4 were waited for; matrix products, arithmetic and copies ran while one was open for 3% of the time, Pallas kernels for 0%

commit v1 on v0

v1 whole, which is shorter than its diff:
```python
import functools
import math

import jax
import jax.numpy as jnp
from jax import lax
from jax.experimental import pallas as pl
from jax.experimental.pallas import tpu as pltpu
from jax.sharding import PartitionSpec as P

MESH = pl.DeviceIdType.MESH
F32 = jnp.float32
BF16 = jnp.bfloat16

first_bias = 1.0 - 0.9**10
second_bias = 1.0 - 0.999**10

PLANES = 8
CHUNKS = 4


def clipped_adam(projected, total, first_moment, second_moment, entries):
    limit = math.sqrt(entries)
    factor = jnp.minimum(1.0, limit / (jnp.sqrt(total) + 1e-06))
    clipped = factor * projected
    first_new = 0.9 * first_moment + 0.1 * clipped
    second_new = 0.999 * second_moment + 0.001 * clipped * clipped
    direction = first_new / first_bias / (jnp.sqrt(second_new / second_bias) + 1e-08)
    return first_new, second_new, direction.astype(BF16)


def step_kernel(
    acts_ref, grad_ref, weight_hbm, basis_ref, first_ref, second_ref,
    grad_in_ref, first_out, second_out, gathered_hbm,
    weight, acts_pair, basis_perm, partial, partial_in, grads, coords,
    own, mine16, arrived, sums_out, sums_in, gathered, back_out, back_in,
    weight_sem, out_sem,
    acts_s, acts_r, coords_s, coords_r, gx_s, gx_r, gc_s, gc_r, gf_s, gf_r,
    rs_s, rs_r, sum_s, sum_r, back_s, back_r,
    az_s, az_r, ax_s, ax_r, ac_s, ac_r, af_s, af_r,
):
    dp = lax.axis_index("dp")
    x = lax.axis_index("fsdp")
    ox = 1 - x
    plane = dp // 2
    core = dp % 2
    oc = 1 - core
    me = core * 2 + x
    tokens, d_in = acts_ref.shape
    half = d_in // 2
    d_out = grad_ref.shape[1]
    wide = d_out // CHUNKS
    rank = basis_ref.shape[1]
    quarter = rank // 4
    rows = rank // (4 * PLANES)

    def device(p, c, f):
        return {"dp": p * 2 + c, "fsdp": f}

    partner = device(plane, core, ox)
    sibling = device(plane, oc, x)
    diagonal = device(plane, oc, ox)
    planes = [device((plane + k) % PLANES, core, x) for k in range(PLANES)]
    group = [partner, sibling, diagonal]

    def send(src, dst, s, r, to):
        copy = pltpu.make_async_remote_copy(
            src_ref=src, dst_ref=dst, send_sem=s, recv_sem=r, device_id=to, device_id_type=MESH
        )
        copy.start()
        return copy

    load = pltpu.make_async_copy(weight_hbm, weight, weight_sem)
    load.start()
    barrier = pltpu.get_barrier_semaphore()
    for to in group + planes[1:]:
        pl.semaphore_signal(barrier, inc=1, device_id=to, device_id_type=MESH)
    pl.semaphore_wait(barrier, 2 + PLANES)

    pending = []
    acts_copy = send(
        acts_ref.at[:, pl.ds(pl.multiple_of(ox * half, half), half)],
        acts_pair.at[x], acts_s, acts_r, partner,
    )
    to_partner = []
    to_sibling = []
    for n in range(CHUNKS):
        cols = pl.ds(n * wide, wide)
        to_partner.append(
            send(grad_ref.at[:, cols], grads.at[me, :, cols], gx_s.at[n], gx_r.at[n], partner)
        )
        to_sibling.append(
            send(grad_ref.at[:, cols], grads.at[me, :, cols], gc_s.at[n], gc_r.at[n], sibling)
        )
    grads[me] = grad_ref[...]

    at = lax.broadcasted_iota(jnp.int32, (rank, rank), 0)
    to = lax.broadcasted_iota(jnp.int32, (rank, rank), 1)
    source = ((to % quarter) // rows * 4 + to // quarter) * rows + to % rows
    shuffle = jnp.where(at == source, 1.0, 0.0).astype(BF16)
    basis_perm[...] = jnp.dot(basis_ref[...], shuffle, preferred_element_type=F32).astype(BF16)

    def project(block):
        return jnp.dot(block, basis_perm[...], preferred_element_type=F32)

    values = project(acts_ref[:, pl.ds(pl.multiple_of(x * half, half), half)])
    for q in range(4):
        partial[q, x] = values[:, q * quarter:(q + 1) * quarter]
    acts_copy.wait_recv()
    values = project(acts_pair[ox])
    for q in range(4):
        partial[q, ox] = values[:, q * quarter:(q + 1) * quarter]
    coord_copies = []
    for k, (to_dev, q) in enumerate(
        [(partner, core * 2 + ox), (diagonal, oc * 2 + ox), (sibling, oc * 2 + x)]
    ):
        coord_copies.append(
            send(partial.at[q], partial_in.at[k], coords_s.at[k], coords_r.at[k], to_dev)
        )
    for copy in coord_copies:
        copy.wait_recv()
    coords[core] = (partial[me] + partial_in[0]).astype(BF16)
    coords[oc] = (partial_in[1] + partial_in[2]).astype(BF16)

    scatter = []
    forward = []
    for n in range(CHUNKS):
        cols = pl.ds(n * wide, wide)
        to_partner[n].wait_recv()
        theirs = core * 2 + ox
        forward.append(
            send(grads.at[theirs, :, cols], grads.at[theirs, :, cols], gf_s.at[n], gf_r.at[n], sibling)
        )
        to_sibling[n].wait_recv()
        forward[n].wait_recv()
        chunk = lax.dot_general(
            coords[...].reshape(4 * tokens, quarter),
            grads[:, :, cols].reshape(4 * tokens, wide),
            (((0,), (0,)), ((), ())),
            preferred_element_type=F32,
        )
        chunk = chunk.reshape(PLANES, rows, wide)
        own[:, :, cols] = chunk
        mine16[:, :, cols] = chunk.astype(BF16)
        for k in range(1, PLANES):
            scatter.append(
                send(
                    mine16.at[(plane + k) % PLANES, :, cols], arrived.at[k - 1, :, cols],
                    rs_s.at[n, k - 1], rs_r.at[n, k - 1], planes[k],
                )
            )

    load.wait()

    def input_gradient(block):
        return lax.dot_general(
            block, weight[...], (((1,), (1,)), ((), ())), preferred_element_type=F32
        ).astype(BF16)

    back_out[...] = input_gradient(grads[core * 2 + ox])
    back = send(back_out, back_in, back_s, back_r, partner)
    grad_in_ref[:, pl.ds(pl.multiple_of(x * half, half), half)] = input_gradient(grad_ref[...])

    for copy in scatter:
        copy.wait_recv()
    projected = own[plane]
    for k in range(PLANES - 1):
        projected = projected + arrived[k].astype(F32)

    sums_out[0] = jnp.full((8, 128), jnp.sum(projected * projected), F32)
    copies = []
    for k in range(1, PLANES):
        copies.append(
            send(sums_out.at[0], sums_in.at[k - 1], sum_s.at[k - 1], sum_r.at[k - 1], planes[k])
        )
    total = sums_out[0]
    for k in range(PLANES - 1):
        copies[k].wait_recv()
        total = total + sums_in[k]
    sums_out[1] = total
    for k, to_dev in enumerate(group):
        j = PLANES - 1 + k
        copies.append(send(sums_out.at[1], sums_in.at[j], sum_s.at[j], sum_r.at[j], to_dev))
    for k in range(3):
        copies[PLANES - 1 + k].wait_recv()
        total = total + sums_in[PLANES - 1 + k]
    pending += copies

    first_new, second_new, direction = clipped_adam(
        projected, total[0:1, 0:1], first_ref[...], second_ref[...], rank * d_out
    )
    gathered[plane, me] = direction
    across = []
    for k in range(1, PLANES):
        block = gathered.at[plane, me]
        across.append(send(block, block, az_s.at[k - 1], az_r.at[k - 1], planes[k]))
    first_out[...] = first_new
    second_out[...] = second_new
    along = []
    siblings = []
    theirs = core * 2 + ox

    def relay(k):
        at_plane = (plane + PLANES - k) % PLANES
        along[k].wait_recv()
        block = gathered.at[at_plane, theirs]
        siblings.append(send(block, block, af_s.at[k], af_r.at[k], sibling))

    for k in range(PLANES):
        if k:
            across[k - 1].wait_recv()
        at_plane = (plane + PLANES - k) % PLANES
        block = gathered.at[at_plane, me]
        along.append(send(block, block, ax_s.at[k], ax_r.at[k], partner))
        siblings.append(send(block, block, ac_s.at[k], ac_r.at[k], sibling))
        if k:
            relay(k - 1)
    relay(PLANES - 1)
    back.wait_recv()
    grad_in_ref[:, pl.ds(pl.multiple_of(ox * half, half), half)] = back_in[...]
    for copy in siblings:
        copy.wait_recv()
    store = pltpu.make_async_copy(gathered, gathered_hbm, out_sem)
    store.start()
    pending += [acts_copy, back] + to_partner + to_sibling + coord_copies + forward
    pending += scatter + across + along + siblings
    for copy in pending:
        copy.wait_send()
    store.wait()


def update_kernel(basis_ref, direction_ref, out_ref):
    update = jnp.dot(basis_ref[...], direction_ref[...], preferred_element_type=F32)
    out_ref[...] = (0.25 * update).astype(BF16)


def on_device_kernel(acts, grad_out, weight, basis, first_moment, second_moment):
    tokens, d_in = acts.shape
    d_out = grad_out.shape[1]
    half = d_in // 2
    rank = basis.shape[1]
    quarter = rank // 4
    rows = rank // (4 * PLANES)
    vmem = pl.BlockSpec(memory_space=pltpu.VMEM)
    anywhere = pl.BlockSpec(memory_space=pl.ANY)
    dma = pltpu.SemaphoreType.DMA
    grad_in, first_new, second_new, direction = pl.pallas_call(
        step_kernel,
        out_shape=(
            jax.ShapeDtypeStruct((tokens, d_in), BF16),
            jax.ShapeDtypeStruct(first_moment.shape, F32),
            jax.ShapeDtypeStruct(second_moment.shape, F32),
            jax.ShapeDtypeStruct((PLANES, 4, rows, d_out), BF16),
        ),
        in_specs=[vmem, vmem, anywhere, vmem, vmem, vmem],
        out_specs=(vmem, vmem, vmem, anywhere),
        scratch_shapes=[
            pltpu.VMEM(weight.shape, BF16),
            pltpu.VMEM((2, tokens, half), BF16),
            pltpu.VMEM(basis.shape, BF16),
            pltpu.VMEM((4, 2, tokens, quarter), F32),
            pltpu.VMEM((3, 2, tokens, quarter), F32),
            pltpu.VMEM((4, tokens, d_out), BF16),
            pltpu.VMEM((2, 2, tokens, quarter), BF16),
            pltpu.VMEM((PLANES, rows, d_out), F32),
            pltpu.VMEM((PLANES, rows, d_out), BF16),
            pltpu.VMEM((PLANES - 1, rows, d_out), BF16),
            pltpu.VMEM((2, 8, 128), F32),
            pltpu.VMEM((PLANES + 2, 8, 128), F32),
            pltpu.VMEM((PLANES, 4, rows, d_out), BF16),
            pltpu.VMEM((tokens, half), BF16),
            pltpu.VMEM((tokens, half), BF16),
            dma, dma,
            dma, dma, dma((3,)), dma((3,)),
            dma((CHUNKS,)), dma((CHUNKS,)), dma((CHUNKS,)), dma((CHUNKS,)),
            dma((CHUNKS,)), dma((CHUNKS,)),
            dma((CHUNKS, PLANES - 1)), dma((CHUNKS, PLANES - 1)),
            dma((PLANES + 2,)), dma((PLANES + 2,)), dma, dma,
            dma((PLANES - 1,)), dma((PLANES - 1,)),
            dma((PLANES,)), dma((PLANES,)), dma((PLANES,)), dma((PLANES,)),
            dma((PLANES,)), dma((PLANES,)),
        ],
        compiler_params=pltpu.CompilerParams(
            collective_id=0, has_side_effects=True, vmem_limit_bytes=48 * 1024 * 1024
        ),
        name="galore_step",
    )(acts, grad_out, weight, basis, first_moment, second_moment)
    direction = direction.reshape(rank, d_out)
    wide = 512
    weight_update = pl.pallas_call(
        update_kernel,
        grid=(d_out // wide,),
        out_shape=jax.ShapeDtypeStruct((basis.shape[0], d_out), BF16),
        in_specs=[
            pl.BlockSpec(basis.shape, lambda j: (0, 0)),
            pl.BlockSpec((rank, wide), lambda j: (0, j)),
        ],
        out_specs=pl.BlockSpec((basis.shape[0], wide), lambda j: (0, j)),
        compiler_params=pltpu.CompilerParams(vmem_limit_bytes=32 * 1024 * 1024),
        name="back_projection",
    )(basis, direction)
    return grad_in, first_new, second_new, weight_update


def on_device(acts, grad_out, weight, basis, first_moment, second_moment):
    grad_in = lax.dot_general(
        grad_out,
        lax.all_gather(weight, "fsdp", axis=0, tiled=True),
        (((1,), (1,)), ((), ())),
        preferred_element_type=F32,
    ).astype(BF16)
    coords = jnp.dot(
        acts, lax.all_gather(basis, "fsdp", axis=0, tiled=True), preferred_element_type=F32
    ).astype(BF16)
    projected = lax.psum_scatter(
        lax.dot_general(coords, grad_out, (((0,), (0,)), ((), ())), preferred_element_type=F32),
        ("dp", "fsdp"),
        scatter_dimension=0,
        tiled=True,
    )
    total = lax.psum(jnp.sum(projected * projected), ("dp", "fsdp"))
    first_new, second_new, direction = clipped_adam(
        projected, total, first_moment, second_moment, basis.shape[1] * grad_out.shape[1]
    )
    update = jnp.dot(
        basis,
        lax.all_gather(direction, ("dp", "fsdp"), axis=0, tiled=True),
        preferred_element_type=F32,
    )
    return grad_in, first_new, second_new, (0.25 * update).astype(BF16)


def solution(mesh):
    split = P(("dp", "fsdp"), None)
    halves = P("fsdp", None)
    small = mesh.shape["dp"] == 2 * PLANES and mesh.shape["fsdp"] == 2
    return jax.shard_map(
        on_device_kernel if small else on_device,
        mesh=mesh,
        in_specs=(split, split, halves, halves, split, split),
        out_specs=(split, split, split, halves),
        check_vma=False,
    )
```

time: 375 us -> 86.7 us (0.23)
  waiting for transfers between devices: 292 us -> 0 us
  Pallas kernels: 0 us -> 78.5 us
  blocking collectives: 39.9 us -> 0 us
  matrix products: 17.9 us -> 0 us
  between operations: 14.5 us -> 0.65 us
    all_gather x3 -> x0, waiting for transfers between devices: 151 us -> none  [the longest x1 61.4 us: on_device(): lax.all_gather(weight, 'fsdp', axis=0, tiled=True)]
    reduce_scatter x1 -> x0, waiting for transfers between devices: 139 us -> none  [on_device(): lax.psum_scatter(lax.dot_general(coords, grad_out, (((0,), (0,)), ((), ()...]
    pallas_call x0 -> x2, Pallas kernels: none -> 78.5 us  [the longest x1 74.3 us: on_device_kernel(): pl.pallas_call(step_kernel, out_shape=(jax.ShapeDtypeStruct((tokens, d_in...]
    psum x1 -> x0, blocking collectives: 39.9 us -> none  [on_device(): total = lax.psum(jnp.sum(projected * projected), ('dp', 'fsdp'))]
    dot_general x3 -> x0, matrix products: 17.9 us -> none  [the longest x1 7.06 us: on_device(): lax.dot_general(grad_out, lax.all_gather(weight, 'fsdp', axis=0, tiled=Tr...]
  transfers between devices with their start and end apart: 4 -> 0, of which waited for: 4 -> 0; matrix products, arithmetic and copies ran while one was open for 3% -> 0% of each run, Pallas kernels for 0% -> 0%
where the time goes in v1:
time: 86.7 us; the launch traced here: 86.4 us
  Pallas kernels  78.5 us (91%)
  local copies, waits for them, and re-layouts  7.21 us (8%)
    pallas_call x1, Pallas kernels, on_device_kernel(): pl.pallas_call(step_kernel, out_shape=(jax.ShapeDtypeStruct((tokens, d_in...  74.3 us
    unnamed x13, local copies, waits for them, and re-layouts  7.21 us
    pallas_call x1, Pallas kernels, on_device_kernel(): pl.pallas_call(update_kernel, grid=(d_out // wide,), out_shape=jax.ShapeD...  4.22 us

profile of v1, /device:TPU:1, one launch (start us, length us, event | category | flops | bytes accessed | tf_op | source)
XLA Modules:
  0.0 86.4 jit_solution(9101719525601323733)
XLA Ops:
  0.6 0.0 copy-start
  0.6 1.2 %copy-done = bf16[1024,512]{1,0:T(8,128)(2,1)S(1)} copy-done((bf16[1024,512]{1,0:T(8,128)(2,1)S(1)}, bf16[1024,512]{1,0:T(8,128)(2,1)}, u32[]{:S(2)}) %copy-start) | copy-done | bytes 1048600
  1.9 0.0 copy-start.1
  1.9 1.0 %copy-done.1 = bf16[128,2048]{1,0:T(8,128)(2,1)S(1)} copy-done((bf16[128,2048]{1,0:T(8,128)(2,1)S(1)}, bf16[128,2048]{1,0:T(8,128)(2,1)}, u32[]{:S(2)}) %copy-start.1) | copy-done | bytes 524312
  2.9 0.0 copy-start.2
  2.9 1.0 %copy-done.2 = bf16[128,2048]{1,0:T(8,128)(2,1)S(1)} copy-done((bf16[128,2048]{1,0:T(8,128)(2,1)S(1)}, bf16[128,2048]{1,0:T(8,128)(2,1)}, u32[]{:S(2)}) %copy-start.2) | copy-done | bytes 524312
  3.9 0.0 copy-start.3
  3.9 0.9 %copy-done.3 = f32[16,2048]{1,0:T(8,128)S(1)} copy-done((f32[16,2048]{1,0:T(8,128)S(1)}, f32[16,2048]{1,0:T(8,128)}, u32[]{:S(2)}) %copy-start.3) | copy-done | bytes 131096
  4.8 0.0 copy-start.4
  4.8 0.9 %copy-done.4 = f32[16,2048]{1,0:T(8,128)S(1)} copy-done((f32[16,2048]{1,0:T(8,128)S(1)}, f32[16,2048]{1,0:T(8,128)}, u32[]{:S(2)}) %copy-start.4) | copy-done | bytes 131096
  5.8 74.3 %galore_step.1 = (bf16[128,2048]{1,0:T(8,128)(2,1)S(1)}, f32[16,2048]{1,0:T(8,128)S(1)}, f32[16,2048]{1,0:T(8,128)S(1)}, bf16[8,4,16,2048]{3,2,1,0:T(8,128)(2,1)S(1)}) custom-call(bf16[128,2048]{1,0:T(8,128)(2,1)S(1)} %copy-done.1, bf16[128,2048]{1,0:T(8,128)(2,1)S(1)} %copy-done.2, bf16[1024,2048]{1,0:T(8,128)(2,1)} %weight_hbm.1, ...), custom_call_target="tpu_custom_call" | custom-call | tf_op jit(solution)/shard_map/galore_step/pallas_call | solution.py:247
  80.1 4.2 %back_projection.1 = bf16[1024,2048]{1,0:T(8,128)(2,1)} custom-call(bf16[1024,512]{1,0:T(8,128)(2,1)S(1)} %copy-done, bf16[512,2048]{1,0:T(8,128)(2,1)S(1)} %bitcast.1), custom_call_target="tpu_custom_call" | custom-call | tf_op jit(solution)/shard_map/back_projection/pallas_call | solution.py:290
  84.3 0.8 copy.13
  85.1 0.7 copy.14
  85.7 0.7 copy.15
Async XLA Ops:
  0.6 1.2 %copy-start = (bf16[1024,512]{1,0:T(8,128)(2,1)S(1)}, bf16[1024,512]{1,0:T(8,128)(2,1)}, u32[]{:S(2)}) copy-start(bf16[1024,512]{1,0:T(8,128)(2,1)} %basis_ref.3) | copy-start | bytes 3145732
  1.9 1.0 %copy-start.1 = (bf16[128,2048]{1,0:T(8,128)(2,1)S(1)}, bf16[128,2048]{1,0:T(8,128)(2,1)}, u32[]{:S(2)}) copy-start(bf16[128,2048]{1,0:T(8,128)(2,1)} %acts_ref.1) | copy-start | bytes 1572868
  2.9 1.0 %copy-start.2 = (bf16[128,2048]{1,0:T(8,128)(2,1)S(1)}, bf16[128,2048]{1,0:T(8,128)(2,1)}, u32[]{:S(2)}) copy-start(bf16[128,2048]{1,0:T(8,128)(2,1)} %grad_ref.1) | copy-start | bytes 1572868
  3.9 0.9 %copy-start.3 = (f32[16,2048]{1,0:T(8,128)S(1)}, f32[16,2048]{1,0:T(8,128)}, u32[]{:S(2)}) copy-start(f32[16,2048]{1,0:T(8,128)} %first_ref.1) | copy-start | bytes 393220
  4.8 0.9 %copy-start.4 = (f32[16,2048]{1,0:T(8,128)S(1)}, f32[16,2048]{1,0:T(8,128)}, u32[]{:S(2)}) copy-start(f32[16,2048]{1,0:T(8,128)} %second_ref.1) | copy-start | bytes 393220

commit v2 on v1

--- a/solution.py
+++ b/solution.py
@@ -30,11 +30,11 @@
 
 
 def step_kernel(
-    acts_ref, grad_ref, weight_hbm, basis_ref, first_ref, second_ref,
+    acts_ref, grad_ref, weight_hbm, basis_hbm, first_hbm, second_hbm,
     grad_in_ref, first_out, second_out, gathered_hbm,
-    weight, acts_pair, basis_perm, partial, partial_in, grads, coords,
+    weight, basis_ref, first_ref, second_ref, acts_pair, basis_perm, partial, partial_in, grads, coords,
     own, mine16, arrived, sums_out, sums_in, gathered, back_out, back_in,
-    weight_sem, out_sem,
+    load_sems, out_sem,
     acts_s, acts_r, coords_s, coords_r, gx_s, gx_r, gc_s, gc_r, gf_s, gf_r,
     rs_s, rs_r, sum_s, sum_r, back_s, back_r,
     az_s, az_r, ax_s, ax_r, ac_s, ac_r, af_s, af_r,
@@ -70,8 +70,14 @@
         copy.start()
         return copy
 
-    load = pltpu.make_async_copy(weight_hbm, weight, weight_sem)
-    load.start()
+    loads = []
+    own_half = acts_ref.at[:, pl.ds(pl.multiple_of(x * half, half), half)]
+    for src, dst in [
+        (basis_hbm, basis_ref), (own_half, acts_pair.at[x]), (grad_ref, grads.at[me]),
+        (first_hbm, first_ref), (second_hbm, second_ref), (weight_hbm, weight),
+    ]:
+        loads.append(pltpu.make_async_copy(src, dst, load_sems.at[len(loads)]))
+        loads[-1].start()
     barrier = pltpu.get_barrier_semaphore()
     for to in group + planes[1:]:
         pl.semaphore_signal(barrier, inc=1, device_id=to, device_id_type=MESH)
@@ -84,26 +90,32 @@
     )
     to_partner = []
     to_sibling = []
-    for n in range(CHUNKS):
+
+    def send_gradient(n):
         cols = pl.ds(n * wide, wide)
         to_partner.append(
             send(grad_ref.at[:, cols], grads.at[me, :, cols], gx_s.at[n], gx_r.at[n], partner)
         )
+
+    send_gradient(0)
+    for n in range(CHUNKS):
+        cols = pl.ds(n * wide, wide)
         to_sibling.append(
             send(grad_ref.at[:, cols], grads.at[me, :, cols], gc_s.at[n], gc_r.at[n], sibling)
         )
-    grads[me] = grad_ref[...]
 
     at = lax.broadcasted_iota(jnp.int32, (rank, rank), 0)
     to = lax.broadcasted_iota(jnp.int32, (rank, rank), 1)
     source = ((to % quarter) // rows * 4 + to // quarter) * rows + to % rows
     shuffle = jnp.where(at == source, 1.0, 0.0).astype(BF16)
+    loads[0].wait()
     basis_perm[...] = jnp.dot(basis_ref[...], shuffle, preferred_element_type=F32).astype(BF16)
 
     def project(block):
         return jnp.dot(block, basis_perm[...], preferred_element_type=F32)
 
-    values = project(acts_ref[:, pl.ds(pl.multiple_of(x * half, half), half)])
+    loads[1].wait()
+    values = project(acts_pair[x])
     for q in range(4):
         partial[q, x] = values[:, q * quarter:(q + 1) * quarter]
     acts_copy.wait_recv()
@@ -117,6 +129,9 @@
         coord_copies.append(
             send(partial.at[q], partial_in.at[k], coords_s.at[k], coords_r.at[k], to_dev)
         )
+    for n in range(1, CHUNKS):
+        send_gradient(n)
+    loads[2].wait()
     for copy in coord_copies:
         copy.wait_recv()
     coords[core] = (partial[me] + partial_in[0]).astype(BF16)
@@ -150,7 +165,7 @@
                 )
             )
 
-    load.wait()
+    loads[5].wait()
 
     def input_gradient(block):
         return lax.dot_general(
@@ -159,8 +174,10 @@
 
     back_out[...] = input_gradient(grads[core * 2 + ox])
     back = send(back_out, back_in, back_s, back_r, partner)
-    grad_in_ref[:, pl.ds(pl.multiple_of(x * half, half), half)] = input_gradient(grad_ref[...])
-
+    grad_in_ref[:, pl.ds(pl.multiple_of(x * half, half), half)] = input_gradient(grads[me])
+
+    loads[3].wait()
+    loads[4].wait()
     for copy in scatter:
         copy.wait_recv()
     projected = own[plane]
@@ -229,7 +246,11 @@
     store.wait()
 
 
-def update_kernel(basis_ref, direction_ref, out_ref):
+def update_kernel(basis_ref, direction_ref, *refs):
+    *results, out_ref = refs
+    kept = len(results) // 2
+    for src, dst in zip(results[:kept], results[kept:]):
+        dst[...] = src[...]
     update = jnp.dot(basis_ref[...], direction_ref[...], preferred_element_type=F32)
     out_ref[...] = (0.25 * update).astype(BF16)
 
@@ -242,7 +263,7 @@
     quarter = rank // 4
     rows = rank // (4 * PLANES)
     vmem = pl.BlockSpec(memory_space=pltpu.VMEM)
-    anywhere = pl.BlockSpec(memory_space=pl.ANY)
+    anywhere = pl.BlockSpec(memory_space=pltpu.HBM)
     dma = pltpu.SemaphoreType.DMA
     grad_in, first_new, second_new, direction = pl.pallas_call(
         step_kernel,
@@ -252,10 +273,13 @@
             jax.ShapeDtypeStruct(second_moment.shape, F32),
             jax.ShapeDtypeStruct((PLANES, 4, rows, d_out), BF16),
         ),
-        in_specs=[vmem, vmem, anywhere, vmem, vmem, vmem],
-        out_specs=(vmem, vmem, vmem, anywhere),
+        in_specs=[anywhere] * 6,
+        out_specs=(vmem, vmem, vmem, pl.BlockSpec(memory_space=pl.ANY)),
         scratch_shapes=[
             pltpu.VMEM(weight.shape, BF16),
+            pltpu.VMEM(basis.shape, BF16),
+            pltpu.VMEM(first_moment.shape, F32),
+            pltpu.VMEM(second_moment.shape, F32),
             pltpu.VMEM((2, tokens, half), BF16),
             pltpu.VMEM(basis.shape, BF16),
             pltpu.VMEM((4, 2, tokens, quarter), F32),
@@ -270,7 +294,7 @@
             pltpu.VMEM((PLANES, 4, rows, d_out), BF16),
             pltpu.VMEM((tokens, half), BF16),
             pltpu.VMEM((tokens, half), BF16),
-            dma, dma,
+            dma((6,)), dma,
             dma, dma, dma((3,)), dma((3,)),
             dma((CHUNKS,)), dma((CHUNKS,)), dma((CHUNKS,)), dma((CHUNKS,)),
             dma((CHUNKS,)), dma((CHUNKS,)),
@@ -281,25 +305,29 @@
             dma((PLANES,)), dma((PLANES,)),
         ],
         compiler_params=pltpu.CompilerParams(
-            collective_id=0, has_side_effects=True, vmem_limit_bytes=48 * 1024 * 1024
+            collective_id=0, has_side_effects=True, vmem_limit_bytes=64 * 1024 * 1024
         ),
         name="galore_step",
     )(acts, grad_out, weight, basis, first_moment, second_moment)
     direction = direction.reshape(rank, d_out)
     wide = 512
-    weight_update = pl.pallas_call(
+    results = (grad_in, first_new, second_new)
+    blocks = [pl.BlockSpec((r.shape[0], wide), lambda j: (0, j)) for r in results]
+    *results, weight_update = pl.pallas_call(
         update_kernel,
         grid=(d_out // wide,),
-        out_shape=jax.ShapeDtypeStruct((basis.shape[0], d_out), BF16),
+        out_shape=[jax.ShapeDtypeStruct(r.shape, r.dtype) for r in results]
+        + [jax.ShapeDtypeStruct((basis.shape[0], d_out), BF16)],
         in_specs=[
             pl.BlockSpec(basis.shape, lambda j: (0, 0)),
             pl.BlockSpec((rank, wide), lambda j: (0, j)),
-        ],
-        out_specs=pl.BlockSpec((basis.shape[0], wide), lambda j: (0, j)),
-        compiler_params=pltpu.CompilerParams(vmem_limit_bytes=32 * 1024 * 1024),
+        ]
+        + blocks,
+        out_specs=blocks + [pl.BlockSpec((basis.shape[0], wide), lambda j: (0, j))],
+        compiler_params=pltpu.CompilerParams(vmem_limit_bytes=64 * 1024 * 1024),
         name="back_projection",
-    )(basis, direction)
-    return grad_in, first_new, second_new, weight_update
+    )(basis, direction, *results)
+    return *results, weight_update
 
 
 def on_device(acts, grad_out, weight, basis, first_moment, second_moment):

time: 86.7 us -> 76.6 us (0.88)
  local copies, waits for them, and re-layouts: 7.21 us -> 0 us
  Pallas kernels: 78.5 us -> 75.8 us
    unnamed x13 -> x0, local copies, waits for them, and re-layouts: 7.21 us -> none
    pallas_call x1, Pallas kernels: 74.3 us -> 69.6 us  [on_device_kernel(): pl.pallas_call(step_kernel, out_shape=(jax.ShapeDtypeStruct((tokens, d_in...]
    pallas_call x1, Pallas kernels: 4.22 us -> 6.21 us  [on_device_kernel(): pl.pallas_call(update_kernel, grid=(d_out // wide,), out_shape=[jax.Shape...]
where the time goes in v2:
time: 76.6 us; the launch traced here: 76.4 us
  Pallas kernels  75.8 us (99%)
    pallas_call x1, Pallas kernels, on_device_kernel(): pl.pallas_call(step_kernel, out_shape=(jax.ShapeDtypeStruct((tokens, d_in...  69.6 us
    pallas_call x1, Pallas kernels, on_device_kernel(): pl.pallas_call(update_kernel, grid=(d_out // wide,), out_shape=[jax.Shape...  6.21 us

profile of v2, /device:TPU:1, one launch (start us, length us, event | category | flops | bytes accessed | tf_op | source)
XLA Modules:
  0.0 76.4 jit_solution(9689372589093369238)
XLA Ops:
  0.6 69.6 %galore_step.1 = (bf16[128,2048]{1,0:T(8,128)(2,1)}, f32[16,2048]{1,0:T(8,128)}, f32[16,2048]{1,0:T(8,128)}, bf16[8,4,16,2048]{3,2,1,0:T(8,128)(2,1)}) custom-call(bf16[128,2048]{1,0:T(8,128)(2,1)} %acts_ref.1, bf16[128,2048]{1,0:T(8,128)(2,1)} %grad_ref.1, bf16[1024,2048]{1,0:T(8,128)(2,1)} %weight_hbm.1, bf16[1024,512]{1,0:T(8,128)(2,1)} %basis_ref.1, ...), custom_call_target="tpu_custom_call" | custom-call | tf_op jit(solution)/shard_map/galore_step/pallas_call | solution.py:268
  70.2 6.2 %back_projection.1 = (bf16[128,2048]{1,0:T(8,128)(2,1)}, f32[16,2048]{1,0:T(8,128)}, f32[16,2048]{1,0:T(8,128)}, bf16[1024,2048]{1,0:T(8,128)(2,1)}) custom-call(bf16[1024,512]{1,0:T(8,128)(2,1)} %basis_ref.1, bf16[512,2048]{1,0:T(8,128)(2,1)} %bitcast.1, bf16[128,2048]{1,0:T(8,128)(2,1)} %get-tuple-element.9.refs_0_, f32[16,2048]{1,0:T(8,128)} %get-tuple-element.10.refs_1_, ...), custom_call_target="tpu_custom_call" | custom-call | tf_op jit(solution)/shard_map/back_projection/pallas_call | solution.py:316

commit v3 on v2

--- a/solution.py
+++ b/solution.py
@@ -16,6 +16,7 @@
 second_bias = 1.0 - 0.999**10
 
 PLANES = 8
+DEPTH = PLANES // 2
 CHUNKS = 4
 
 
@@ -33,11 +34,11 @@
     acts_ref, grad_ref, weight_hbm, basis_hbm, first_hbm, second_hbm,
     grad_in_ref, first_out, second_out, gathered_hbm,
     weight, basis_ref, first_ref, second_ref, acts_pair, basis_perm, partial, partial_in, grads, coords,
-    own, mine16, arrived, sums_out, sums_in, gathered, back_out, back_in,
+    feature, own, mine16, arrived, sums_out, sums_in, gathered, back_out, back_in,
     load_sems, out_sem,
     acts_s, acts_r, coords_s, coords_r, gx_s, gx_r, gc_s, gc_r, gf_s, gf_r,
     rs_s, rs_r, sum_s, sum_r, back_s, back_r,
-    az_s, az_r, ax_s, ax_r, ac_s, ac_r, af_s, af_r,
+    gather_s, gather_r,
 ):
     dp = lax.axis_index("dp")
     x = lax.axis_index("fsdp")
@@ -137,6 +138,7 @@
     coords[core] = (partial[me] + partial_in[0]).astype(BF16)
     coords[oc] = (partial_in[1] + partial_in[2]).astype(BF16)
 
+    loads[5].wait()
     scatter = []
     forward = []
     for n in range(CHUNKS):
@@ -164,17 +166,20 @@
                     rs_s.at[n, k - 1], rs_r.at[n, k - 1], planes[k],
                 )
             )
-
-    loads[5].wait()
-
-    def input_gradient(block):
-        return lax.dot_general(
-            block, weight[...], (((1,), (1,)), ((), ())), preferred_element_type=F32
-        ).astype(BF16)
-
-    back_out[...] = input_gradient(grads[core * 2 + ox])
+        term = lax.dot_general(
+            grads[pl.ds(core * 2, 2), :, cols].reshape(2 * tokens, wide),
+            weight[:, cols],
+            (((1,), (1,)), ((), ())),
+            preferred_element_type=F32,
+        ).reshape(2, tokens, half)
+        if n == 0:
+            feature[...] = term
+        else:
+            feature[...] += term
+
+    back_out[...] = feature[ox].astype(BF16)
     back = send(back_out, back_in, back_s, back_r, partner)
-    grad_in_ref[:, pl.ds(pl.multiple_of(x * half, half), half)] = input_gradient(grads[me])
+    grad_in_ref[:, pl.ds(pl.multiple_of(x * half, half), half)] = feature[x].astype(BF16)
 
     loads[3].wait()
     loads[4].wait()
@@ -185,62 +190,84 @@
         projected = projected + arrived[k].astype(F32)
 
     sums_out[0] = jnp.full((8, 128), jnp.sum(projected * projected), F32)
-    copies = []
+    sums = []
     for k in range(1, PLANES):
-        copies.append(
+        sums.append(
             send(sums_out.at[0], sums_in.at[k - 1], sum_s.at[k - 1], sum_r.at[k - 1], planes[k])
         )
     total = sums_out[0]
     for k in range(PLANES - 1):
-        copies[k].wait_recv()
+        sums[k].wait_recv()
         total = total + sums_in[k]
     sums_out[1] = total
     for k, to_dev in enumerate(group):
         j = PLANES - 1 + k
-        copies.append(send(sums_out.at[1], sums_in.at[j], sum_s.at[j], sum_r.at[j], to_dev))
+        sums.append(send(sums_out.at[1], sums_in.at[j], sum_s.at[j], sum_r.at[j], to_dev))
     for k in range(3):
-        copies[PLANES - 1 + k].wait_recv()
+        sums[PLANES - 1 + k].wait_recv()
         total = total + sums_in[PLANES - 1 + k]
-    pending += copies
+    pending += sums
 
     first_new, second_new, direction = clipped_adam(
         projected, total[0:1, 0:1], first_ref[...], second_ref[...], rank * d_out
     )
     gathered[plane, me] = direction
-    across = []
-    for k in range(1, PLANES):
-        block = gathered.at[plane, me]
-        across.append(send(block, block, az_s.at[k - 1], az_r.at[k - 1], planes[k]))
+    z = plane // 2
+    y = plane % 2
+    oy = 1 - y
+    theirs = core * 2 + ox
+    beside = device(z * 2 + oy, core, x)
+    left = pl.ds(0, d_out // 2)
+    right = pl.ds(d_out // 2, d_out // 2)
+    copies = {}
+
+    def pass_on(kind, j, block, to_dev):
+        copies[kind, j] = send(block, block, gather_s.at[kind, j], gather_r.at[kind, j], to_dev)
+
+    for j in range(1, DEPTH):
+        pass_on(0, j, gathered.at[plane, me], device((z + j) % DEPTH * 2 + y, core, x))
+
+    def spread(j):
+        if j:
+            copies[0, j].wait_recv()
+        block = gathered.at[(z + DEPTH - j) % DEPTH * 2 + y, me]
+        pass_on(1, j, block, beside)
+        pass_on(2, j, block, partner)
+        pass_on(3, j, block, sibling)
+
+    def relay(j):
+        at_z = (z + DEPTH - j) % DEPTH * 2
+        copies[1, j].wait_recv()
+        pass_on(4, j, gathered.at[at_z + oy, me, :, left], partner)
+        pass_on(5, j, gathered.at[at_z + oy, me], sibling)
+        copies[2, j].wait_recv()
+        pass_on(6, j, gathered.at[at_z + y, theirs, :, right], beside)
+        pass_on(7, j, gathered.at[at_z + y, theirs], sibling)
+
+    def corner(j):
+        copies[4, j].wait_recv()
+        copies[6, j].wait_recv()
+        pass_on(8, j, gathered.at[(z + DEPTH - j) % DEPTH * 2 + oy, theirs], sibling)
+
+    spread(0)
     first_out[...] = first_new
     second_out[...] = second_new
-    along = []
-    siblings = []
-    theirs = core * 2 + ox
-
-    def relay(k):
-        at_plane = (plane + PLANES - k) % PLANES
-        along[k].wait_recv()
-        block = gathered.at[at_plane, theirs]
-        siblings.append(send(block, block, af_s.at[k], af_r.at[k], sibling))
-
-    for k in range(PLANES):
-        if k:
-            across[k - 1].wait_recv()
-        at_plane = (plane + PLANES - k) % PLANES
-        block = gathered.at[at_plane, me]
-        along.append(send(block, block, ax_s.at[k], ax_r.at[k], partner))
-        siblings.append(send(block, block, ac_s.at[k], ac_r.at[k], sibling))
-        if k:
-            relay(k - 1)
-    relay(PLANES - 1)
+    for j in range(1, DEPTH + 2):
+        if j < DEPTH:
+            spread(j)
+        if j <= DEPTH:
+            relay(j - 1)
+        if j >= 2:
+            corner(j - 2)
     back.wait_recv()
     grad_in_ref[:, pl.ds(pl.multiple_of(ox * half, half), half)] = back_in[...]
-    for copy in siblings:
-        copy.wait_recv()
+    for kind in (3, 5, 7, 8):
+        for j in range(DEPTH):
+            copies[kind, j].wait_recv()
     store = pltpu.make_async_copy(gathered, gathered_hbm, out_sem)
     store.start()
     pending += [acts_copy, back] + to_partner + to_sibling + coord_copies + forward
-    pending += scatter + across + along + siblings
+    pending += scatter + list(copies.values())
     for copy in pending:
         copy.wait_send()
     store.wait()
@@ -286,6 +313,7 @@
             pltpu.VMEM((3, 2, tokens, quarter), F32),
             pltpu.VMEM((4, tokens, d_out), BF16),
             pltpu.VMEM((2, 2, tokens, quarter), BF16),
+            pltpu.VMEM((2, tokens, half), F32),
             pltpu.VMEM((PLANES, rows, d_out), F32),
             pltpu.VMEM((PLANES, rows, d_out), BF16),
             pltpu.VMEM((PLANES - 1, rows, d_out), BF16),
@@ -300,9 +328,7 @@
             dma((CHUNKS,)), dma((CHUNKS,)),
             dma((CHUNKS, PLANES - 1)), dma((CHUNKS, PLANES - 1)),
             dma((PLANES + 2,)), dma((PLANES + 2,)), dma, dma,
-            dma((PLANES - 1,)), dma((PLANES - 1,)),
-            dma((PLANES,)), dma((PLANES,)), dma((PLANES,)), dma((PLANES,)),
-            dma((PLANES,)), dma((PLANES,)),
+            dma((9, DEPTH)), dma((9, DEPTH)),
         ],
         compiler_params=pltpu.CompilerParams(
             collective_id=0, has_side_effects=True, vmem_limit_bytes=64 * 1024 * 1024

time: 76.6 us -> 71.6 us (0.935)
  Pallas kernels: 75.8 us -> 70.7 us
    pallas_call x1, Pallas kernels: 69.6 us -> 64.5 us  [on_device_kernel(): pl.pallas_call(step_kernel, out_shape=(jax.ShapeDtypeStruct((tokens, d_in...]
where the time goes in v3:
time: 71.6 us; the launch traced here: 71.4 us
  Pallas kernels  70.7 us (99%)
    pallas_call x1, Pallas kernels, on_device_kernel(): pl.pallas_call(step_kernel, out_shape=(jax.ShapeDtypeStruct((tokens, d_in...  64.5 us
    pallas_call x1, Pallas kernels, on_device_kernel(): pl.pallas_call(update_kernel, grid=(d_out // wide,), out_shape=[jax.Shape...  6.22 us

profile of v3, /device:TPU:1, one launch (start us, length us, event | category | flops | bytes accessed | tf_op | source)
XLA Modules:
  0.0 71.4 jit_solution(3440724253627933147)
XLA Ops:
  0.6 64.5 %galore_step.1 = (bf16[128,2048]{1,0:T(8,128)(2,1)}, f32[16,2048]{1,0:T(8,128)}, f32[16,2048]{1,0:T(8,128)}, bf16[8,4,16,2048]{3,2,1,0:T(8,128)(2,1)}) custom-call(bf16[128,2048]{1,0:T(8,128)(2,1)} %acts_ref.1, bf16[128,2048]{1,0:T(8,128)(2,1)} %grad_ref.1, bf16[1024,2048]{1,0:T(8,128)(2,1)} %weight_hbm.1, bf16[1024,512]{1,0:T(8,128)(2,1)} %basis_ref.1, ...), custom_call_target="tpu_custom_call" | custom-call | tf_op jit(solution)/shard_map/galore_step/pallas_call | solution.py:295
  65.1 6.2 %back_projection.1 = (bf16[128,2048]{1,0:T(8,128)(2,1)}, f32[16,2048]{1,0:T(8,128)}, f32[16,2048]{1,0:T(8,128)}, bf16[1024,2048]{1,0:T(8,128)(2,1)}) custom-call(bf16[1024,512]{1,0:T(8,128)(2,1)} %basis_ref.1, bf16[512,2048]{1,0:T(8,128)(2,1)} %bitcast.1, bf16[128,2048]{1,0:T(8,128)(2,1)} %get-tuple-element.9.refs_0_, f32[16,2048]{1,0:T(8,128)} %get-tuple-element.10.refs_1_, ...), custom_call_target="tpu_custom_call" | custom-call | tf_op jit(solution)/shard_map/back_projection/pallas_call | solution.py:342

commit v4 on v3

--- a/solution.py
+++ b/solution.py
@@ -34,10 +34,10 @@
     acts_ref, grad_ref, weight_hbm, basis_hbm, first_hbm, second_hbm,
     grad_in_ref, first_out, second_out, gathered_hbm,
     weight, basis_ref, first_ref, second_ref, acts_pair, basis_perm, partial, partial_in, grads, coords,
-    feature, own, mine16, arrived, sums_out, sums_in, gathered, back_out, back_in,
+    feature, own, mine16, from_y, pairs, pairs16, arrived, sums_out, sums_in, gathered, back_out, back_in,
     load_sems, out_sem,
     acts_s, acts_r, coords_s, coords_r, gx_s, gx_r, gc_s, gc_r, gf_s, gf_r,
-    rs_s, rs_r, sum_s, sum_r, back_s, back_r,
+    ry_s, ry_r, rs_s, rs_r, sum_s, sum_r, back_s, back_r,
     gather_s, gather_r,
 ):
     dp = lax.axis_index("dp")
@@ -98,7 +98,6 @@
             send(grad_ref.at[:, cols], grads.at[me, :, cols], gx_s.at[n], gx_r.at[n], partner)
         )
 
-    send_gradient(0)
     for n in range(CHUNKS):
         cols = pl.ds(n * wide, wide)
         to_sibling.append(
@@ -119,6 +118,8 @@
     values = project(acts_pair[x])
     for q in range(4):
         partial[q, x] = values[:, q * quarter:(q + 1) * quarter]
+    acts_copy.wait_send()
+    send_gradient(0)
     acts_copy.wait_recv()
     values = project(acts_pair[ox])
     for q in range(4):
@@ -130,20 +131,42 @@
         coord_copies.append(
             send(partial.at[q], partial_in.at[k], coords_s.at[k], coords_r.at[k], to_dev)
         )
-    for n in range(1, CHUNKS):
-        send_gradient(n)
+    send_gradient(1)
     loads[2].wait()
     for copy in coord_copies:
         copy.wait_recv()
+    send_gradient(2)
     coords[core] = (partial[me] + partial_in[0]).astype(BF16)
     coords[oc] = (partial_in[1] + partial_in[2]).astype(BF16)
 
     loads[5].wait()
+    z = plane // 2
+    y = plane % 2
+    oy = 1 - y
+    beside = device(z * 2 + oy, core, x)
+    over_y = []
     scatter = []
     forward = []
+
+    def reduce_z(n):
+        cols = pl.ds(n * wide, wide)
+        over_y[n].wait_recv()
+        pair = own[:, y, :, cols] + from_y[:, :, cols].astype(F32)
+        pairs[:, :, cols] = pair
+        pairs16[:, :, cols] = pair.astype(BF16)
+        for k in range(1, DEPTH):
+            scatter.append(
+                send(
+                    pairs16.at[(z + k) % DEPTH, :, cols], arrived.at[k - 1, :, cols],
+                    rs_s.at[n, k - 1], rs_r.at[n, k - 1], device((z + k) % DEPTH * 2 + y, core, x),
+                )
+            )
+
     for n in range(CHUNKS):
         cols = pl.ds(n * wide, wide)
         to_partner[n].wait_recv()
+        if n + 3 < CHUNKS:
+            send_gradient(n + 3)
         theirs = core * 2 + ox
         forward.append(
             send(grads.at[theirs, :, cols], grads.at[theirs, :, cols], gf_s.at[n], gf_r.at[n], sibling)
@@ -156,16 +179,16 @@
             (((0,), (0,)), ((), ())),
             preferred_element_type=F32,
         )
-        chunk = chunk.reshape(PLANES, rows, wide)
-        own[:, :, cols] = chunk
-        mine16[:, :, cols] = chunk.astype(BF16)
-        for k in range(1, PLANES):
-            scatter.append(
-                send(
-                    mine16.at[(plane + k) % PLANES, :, cols], arrived.at[k - 1, :, cols],
-                    rs_s.at[n, k - 1], rs_r.at[n, k - 1], planes[k],
-                )
+        chunk = chunk.reshape(DEPTH, 2, rows, wide)
+        own[:, :, :, cols] = chunk
+        mine16[:, :, :, cols] = chunk.astype(BF16)
+        over_y.append(
+            send(
+                mine16.at[:, oy, :, cols], from_y.at[:, :, cols], ry_s.at[n], ry_r.at[n], beside
             )
+        )
+        if n:
+            reduce_z(n - 1)
         term = lax.dot_general(
             grads[pl.ds(core * 2, 2), :, cols].reshape(2 * tokens, wide),
             weight[:, cols],
@@ -177,6 +200,7 @@
         else:
             feature[...] += term
 
+    reduce_z(CHUNKS - 1)
     back_out[...] = feature[ox].astype(BF16)
     back = send(back_out, back_in, back_s, back_r, partner)
     grad_in_ref[:, pl.ds(pl.multiple_of(x * half, half), half)] = feature[x].astype(BF16)
@@ -185,8 +209,8 @@
     loads[4].wait()
     for copy in scatter:
         copy.wait_recv()
-    projected = own[plane]
-    for k in range(PLANES - 1):
+    projected = pairs[z]
+    for k in range(DEPTH - 1):
         projected = projected + arrived[k].astype(F32)
 
     sums_out[0] = jnp.full((8, 128), jnp.sum(projected * projected), F32)
@@ -212,11 +236,7 @@
         projected, total[0:1, 0:1], first_ref[...], second_ref[...], rank * d_out
     )
     gathered[plane, me] = direction
-    z = plane // 2
-    y = plane % 2
-    oy = 1 - y
     theirs = core * 2 + ox
-    beside = device(z * 2 + oy, core, x)
     left = pl.ds(0, d_out // 2)
     right = pl.ds(d_out // 2, d_out // 2)
     copies = {}
@@ -266,8 +286,8 @@
             copies[kind, j].wait_recv()
     store = pltpu.make_async_copy(gathered, gathered_hbm, out_sem)
     store.start()
-    pending += [acts_copy, back] + to_partner + to_sibling + coord_copies + forward
-    pending += scatter + list(copies.values())
+    pending += [back] + to_partner + to_sibling + coord_copies + forward
+    pending += over_y + scatter + list(copies.values())
     for copy in pending:
         copy.wait_send()
     store.wait()
@@ -314,9 +334,12 @@
             pltpu.VMEM((4, tokens, d_out), BF16),
             pltpu.VMEM((2, 2, tokens, quarter), BF16),
             pltpu.VMEM((2, tokens, half), F32),
-            pltpu.VMEM((PLANES, rows, d_out), F32),
-            pltpu.VMEM((PLANES, rows, d_out), BF16),
-            pltpu.VMEM((PLANES - 1, rows, d_out), BF16),
+            pltpu.VMEM((DEPTH, 2, rows, d_out), F32),
+            pltpu.VMEM((DEPTH, 2, rows, d_out), BF16),
+            pltpu.VMEM((DEPTH, rows, d_out), BF16),
+            pltpu.VMEM((DEPTH, rows, d_out), F32),
+            pltpu.VMEM((DEPTH, rows, d_out), BF16),
+            pltpu.VMEM((DEPTH - 1, rows, d_out), BF16),
             pltpu.VMEM((2, 8, 128), F32),
             pltpu.VMEM((PLANES + 2, 8, 128), F32),
             pltpu.VMEM((PLANES, 4, rows, d_out), BF16),
@@ -326,7 +349,8 @@
             dma, dma, dma((3,)), dma((3,)),
             dma((CHUNKS,)), dma((CHUNKS,)), dma((CHUNKS,)), dma((CHUNKS,)),
             dma((CHUNKS,)), dma((CHUNKS,)),
-            dma((CHUNKS, PLANES - 1)), dma((CHUNKS, PLANES - 1)),
+            dma((CHUNKS,)), dma((CHUNKS,)),
+            dma((CHUNKS, DEPTH - 1)), dma((CHUNKS, DEPTH - 1)),
             dma((PLANES + 2,)), dma((PLANES + 2,)), dma, dma,
             dma((9, DEPTH)), dma((9, DEPTH)),
         ],

time: 71.6 us -> 72.6 us (1.014)
  Pallas kernels: 70.7 us -> 71.7 us
    pallas_call x1, Pallas kernels: 64.5 us -> 65.5 us  [on_device_kernel(): pl.pallas_call(step_kernel, out_shape=(jax.ShapeDtypeStruct((tokens, d_in...]
where the time goes in v4:
time: 72.6 us; the launch traced here: 72.4 us
  Pallas kernels  71.7 us (99%)
    pallas_call x1, Pallas kernels, on_device_kernel(): pl.pallas_call(step_kernel, out_shape=(jax.ShapeDtypeStruct((tokens, d_in...  65.5 us
    pallas_call x1, Pallas kernels, on_device_kernel(): pl.pallas_call(update_kernel, grid=(d_out // wide,), out_shape=[jax.Shape...  6.22 us

profile of v4, /device:TPU:1, one launch (start us, length us, event | category | flops | bytes accessed | tf_op | source)
XLA Modules:
  0.0 72.4 jit_solution(1143564954874871203)
XLA Ops:
  0.6 65.5 %galore_step.1 = (bf16[128,2048]{1,0:T(8,128)(2,1)}, f32[16,2048]{1,0:T(8,128)}, f32[16,2048]{1,0:T(8,128)}, bf16[8,4,16,2048]{3,2,1,0:T(8,128)(2,1)}) custom-call(bf16[128,2048]{1,0:T(8,128)(2,1)} %acts_ref.1, bf16[128,2048]{1,0:T(8,128)(2,1)} %grad_ref.1, bf16[1024,2048]{1,0:T(8,128)(2,1)} %weight_hbm.1, bf16[1024,512]{1,0:T(8,128)(2,1)} %basis_ref.1, ...), custom_call_target="tpu_custom_call" | custom-call | tf_op jit(solution)/shard_map/galore_step/pallas_call | solution.py:315
  66.1 6.2 %back_projection.1 = (bf16[128,2048]{1,0:T(8,128)(2,1)}, f32[16,2048]{1,0:T(8,128)}, f32[16,2048]{1,0:T(8,128)}, bf16[1024,2048]{1,0:T(8,128)(2,1)}) custom-call(bf16[1024,512]{1,0:T(8,128)(2,1)} %basis_ref.1, bf16[512,2048]{1,0:T(8,128)(2,1)} %bitcast.1, bf16[128,2048]{1,0:T(8,128)(2,1)} %get-tuple-element.9.refs_0_, f32[16,2048]{1,0:T(8,128)} %get-tuple-element.10.refs_1_, ...), custom_call_target="tpu_custom_call" | custom-call | tf_op jit(solution)/shard_map/back_projection/pallas_call | solution.py:366

commit v5 on v4

--- a/solution.py
+++ b/solution.py
@@ -17,6 +17,7 @@
 
 PLANES = 8
 DEPTH = PLANES // 2
+SUBS = 2
 CHUNKS = 4
 
 
@@ -33,10 +34,10 @@
 def step_kernel(
     acts_ref, grad_ref, weight_hbm, basis_hbm, first_hbm, second_hbm,
     grad_in_ref, first_out, second_out, gathered_hbm,
-    weight, basis_ref, first_ref, second_ref, acts_pair, basis_perm, partial, partial_in, grads, coords,
+    weight, basis_all, acts_own, first_ref, second_ref, coords_out, grads, coords,
     feature, own, mine16, from_y, pairs, pairs16, arrived, sums_out, sums_in, gathered, back_out, back_in,
     load_sems, out_sem,
-    acts_s, acts_r, coords_s, coords_r, gx_s, gx_r, gc_s, gc_r, gf_s, gf_r,
+    basis_s, basis_r, coords_s, coords_r, gx_s, gx_r, gc_s, gc_r, gf_s, gf_r,
     ry_s, ry_r, rs_s, rs_r, sum_s, sum_r, back_s, back_r,
     gather_s, gather_r,
 ):
@@ -51,7 +52,8 @@
     half = d_in // 2
     d_out = grad_ref.shape[1]
     wide = d_out // CHUNKS
-    rank = basis_ref.shape[1]
+    rank = basis_hbm.shape[1]
+    piece = half // (4 * SUBS)
     quarter = rank // 4
     rows = rank // (4 * PLANES)
 
@@ -61,6 +63,10 @@
     partner = device(plane, core, ox)
     sibling = device(plane, oc, x)
     diagonal = device(plane, oc, ox)
+    z = plane // 2
+    y = plane % 2
+    oy = 1 - y
+    beside = device(z * 2 + oy, core, x)
     planes = [device((plane + k) % PLANES, core, x) for k in range(PLANES)]
     group = [partner, sibling, diagonal]
 
@@ -72,9 +78,8 @@
         return copy
 
     loads = []
-    own_half = acts_ref.at[:, pl.ds(pl.multiple_of(x * half, half), half)]
     for src, dst in [
-        (basis_hbm, basis_ref), (own_half, acts_pair.at[x]), (grad_ref, grads.at[me]),
+        (basis_hbm, basis_all.at[x]), (acts_ref, acts_own), (grad_ref, grads.at[me]),
         (first_hbm, first_ref), (second_hbm, second_ref), (weight_hbm, weight),
     ]:
         loads.append(pltpu.make_async_copy(src, dst, load_sems.at[len(loads)]))
@@ -85,10 +90,17 @@
     pl.semaphore_wait(barrier, 2 + PLANES)
 
     pending = []
-    acts_copy = send(
-        acts_ref.at[:, pl.ds(pl.multiple_of(ox * half, half), half)],
-        acts_pair.at[x], acts_s, acts_r, partner,
-    )
+    basis_copies = {}
+
+    def basis_rows(quarter_at, i):
+        return pl.ds(pl.multiple_of((quarter_at * SUBS + i) * piece, piece), piece)
+
+    def pass_basis(kind, i, src, dst, to_dev):
+        basis_copies[kind, i] = send(src, dst, basis_s.at[kind, i], basis_r.at[kind, i], to_dev)
+
+    for i in range(SUBS):
+        at = basis_rows(y * 2 + core, i)
+        pass_basis(0, i, basis_hbm.at[at], basis_all.at[x, at], partner)
     to_partner = []
     to_sibling = []
 
@@ -98,6 +110,7 @@
             send(grad_ref.at[:, cols], grads.at[me, :, cols], gx_s.at[n], gx_r.at[n], partner)
         )
 
+    send_gradient(0)
     for n in range(CHUNKS):
         cols = pl.ds(n * wide, wide)
         to_sibling.append(
@@ -108,42 +121,50 @@
     to = lax.broadcasted_iota(jnp.int32, (rank, rank), 1)
     source = ((to % quarter) // rows * 4 + to // quarter) * rows + to % rows
     shuffle = jnp.where(at == source, 1.0, 0.0).astype(BF16)
+
     loads[0].wait()
-    basis_perm[...] = jnp.dot(basis_ref[...], shuffle, preferred_element_type=F32).astype(BF16)
-
-    def project(block):
-        return jnp.dot(block, basis_perm[...], preferred_element_type=F32)
-
     loads[1].wait()
-    values = project(acts_pair[x])
+    values = jnp.dot(
+        acts_own[:, pl.ds(pl.multiple_of(x * half, half), half)],
+        basis_all[x],
+        preferred_element_type=F32,
+    )
+    for i in range(SUBS):
+        basis_copies[0, i].wait_recv()
+        at = basis_rows(y * 2 + core, i)
+        block = basis_all.at[ox, at]
+        pass_basis(1, i, block, block, beside)
+        pass_basis(2, i, block, block, sibling)
+    for n in range(1, CHUNKS):
+        send_gradient(n)
+    for i in range(SUBS):
+        basis_copies[1, i].wait_recv()
+        block = basis_all.at[ox, basis_rows(oy * 2 + core, i)]
+        pass_basis(3, i, block, block, sibling)
+    for kind in (2, 3):
+        for i in range(SUBS):
+            basis_copies[kind, i].wait_recv()
+    values += jnp.dot(
+        acts_own[:, pl.ds(pl.multiple_of(ox * half, half), half)],
+        basis_all[ox],
+        preferred_element_type=F32,
+    )
+    values = jnp.dot(values.astype(BF16), shuffle, preferred_element_type=F32).astype(BF16)
     for q in range(4):
-        partial[q, x] = values[:, q * quarter:(q + 1) * quarter]
-    acts_copy.wait_send()
-    send_gradient(0)
-    acts_copy.wait_recv()
-    values = project(acts_pair[ox])
-    for q in range(4):
-        partial[q, ox] = values[:, q * quarter:(q + 1) * quarter]
+        coords_out[q] = values[:, q * quarter:(q + 1) * quarter]
     coord_copies = []
     for k, (to_dev, q) in enumerate(
         [(partner, core * 2 + ox), (diagonal, oc * 2 + ox), (sibling, oc * 2 + x)]
     ):
         coord_copies.append(
-            send(partial.at[q], partial_in.at[k], coords_s.at[k], coords_r.at[k], to_dev)
-        )
-    send_gradient(1)
+            send(coords_out.at[q], coords.at[me], coords_s.at[k], coords_r.at[k], to_dev)
+        )
+    coords[me] = coords_out[me]
     loads[2].wait()
     for copy in coord_copies:
         copy.wait_recv()
-    send_gradient(2)
-    coords[core] = (partial[me] + partial_in[0]).astype(BF16)
-    coords[oc] = (partial_in[1] + partial_in[2]).astype(BF16)
 
     loads[5].wait()
-    z = plane // 2
-    y = plane % 2
-    oy = 1 - y
-    beside = device(z * 2 + oy, core, x)
     over_y = []
     scatter = []
     forward = []
@@ -165,8 +186,6 @@
     for n in range(CHUNKS):
         cols = pl.ds(n * wide, wide)
         to_partner[n].wait_recv()
-        if n + 3 < CHUNKS:
-            send_gradient(n + 3)
         theirs = core * 2 + ox
         forward.append(
             send(grads.at[theirs, :, cols], grads.at[theirs, :, cols], gf_s.at[n], gf_r.at[n], sibling)
@@ -286,7 +305,7 @@
             copies[kind, j].wait_recv()
     store = pltpu.make_async_copy(gathered, gathered_hbm, out_sem)
     store.start()
-    pending += [back] + to_partner + to_sibling + coord_copies + forward
+    pending += [back] + list(basis_copies.values()) + to_partner + to_sibling + coord_copies + forward
     pending += over_y + scatter + list(copies.values())
     for copy in pending:
         copy.wait_send()
@@ -324,15 +343,13 @@
         out_specs=(vmem, vmem, vmem, pl.BlockSpec(memory_space=pl.ANY)),
         scratch_shapes=[
             pltpu.VMEM(weight.shape, BF16),
-            pltpu.VMEM(basis.shape, BF16),
+            pltpu.VMEM((2,) + basis.shape, BF16),
+            pltpu.VMEM(acts.shape, BF16),
             pltpu.VMEM(first_moment.shape, F32),
             pltpu.VMEM(second_moment.shape, F32),
-            pltpu.VMEM((2, tokens, half), BF16),
-            pltpu.VMEM(basis.shape, BF16),
-            pltpu.VMEM((4, 2, tokens, quarter), F32),
-            pltpu.VMEM((3, 2, tokens, quarter), F32),
+            pltpu.VMEM((4, tokens, quarter), BF16),
             pltpu.VMEM((4, tokens, d_out), BF16),
-            pltpu.VMEM((2, 2, tokens, quarter), BF16),
+            pltpu.VMEM((4, tokens, quarter), BF16),
             pltpu.VMEM((2, tokens, half), F32),
             pltpu.VMEM((DEPTH, 2, rows, d_out), F32),
             pltpu.VMEM((DEPTH, 2, rows, d_out), BF16),
@@ -346,7 +363,7 @@
             pltpu.VMEM((tokens, half), BF16),
             pltpu.VMEM((tokens, half), BF16),
             dma((6,)), dma,
-            dma, dma, dma((3,)), dma((3,)),
+            dma((4, SUBS)), dma((4, SUBS)), dma((3,)), dma((3,)),
             dma((CHUNKS,)), dma((CHUNKS,)), dma((CHUNKS,)), dma((CHUNKS,)),
             dma((CHUNKS,)), dma((CHUNKS,)),
             dma((CHUNKS,)), dma((CHUNKS,)),

time: 72.6 us -> 75.1 us (1.034)
  Pallas kernels: 71.7 us -> 74.3 us
    pallas_call x1, Pallas kernels: 65.5 us -> 68.1 us  [on_device_kernel(): pl.pallas_call(step_kernel, out_shape=(jax.ShapeDtypeStruct((tokens, d_in...]
where the time goes in v5:
time: 75.1 us; the launch traced here: 74.9 us
  Pallas kernels  74.3 us (99%)
    pallas_call x1, Pallas kernels, on_device_kernel(): pl.pallas_call(step_kernel, out_shape=(jax.ShapeDtypeStruct((tokens, d_in...  68.1 us
    pallas_call x1, Pallas kernels, on_device_kernel(): pl.pallas_call(update_kernel, grid=(d_out // wide,), out_shape=[jax.Shape...  6.21 us

profile of v5, /device:TPU:1, one launch (start us, length us, event | category | flops | bytes accessed | tf_op | source)
XLA Modules:
  0.0 74.9 jit_solution(9493197581813536069)
XLA Ops:
  0.6 68.1 %galore_step.1 = (bf16[128,2048]{1,0:T(8,128)(2,1)}, f32[16,2048]{1,0:T(8,128)}, f32[16,2048]{1,0:T(8,128)}, bf16[8,4,16,2048]{3,2,1,0:T(8,128)(2,1)}) custom-call(bf16[128,2048]{1,0:T(8,128)(2,1)} %acts_ref.1, bf16[128,2048]{1,0:T(8,128)(2,1)} %grad_ref.1, bf16[1024,2048]{1,0:T(8,128)(2,1)} %weight_hbm.1, bf16[1024,512]{1,0:T(8,128)(2,1)} %basis_ref.1, ...), custom_call_target="tpu_custom_call" | custom-call | tf_op jit(solution)/shard_map/galore_step/pallas_call | solution.py:334
  68.7 6.2 %back_projection.1 = (bf16[128,2048]{1,0:T(8,128)(2,1)}, f32[16,2048]{1,0:T(8,128)}, f32[16,2048]{1,0:T(8,128)}, bf16[1024,2048]{1,0:T(8,128)(2,1)}) custom-call(bf16[1024,512]{1,0:T(8,128)(2,1)} %basis_ref.1, bf16[512,2048]{1,0:T(8,128)(2,1)} %bitcast.1, bf16[128,2048]{1,0:T(8,128)(2,1)} %get-tuple-element.9.refs_0_, f32[16,2048]{1,0:T(8,128)} %get-tuple-element.10.refs_1_, ...), custom_call_target="tpu_custom_call" | custom-call | tf_op jit(solution)/shard_map/back_projection/pallas_call | solution.py:383

commit v6 on v4

--- a/solution.py
+++ b/solution.py
@@ -98,6 +98,7 @@
             send(grad_ref.at[:, cols], grads.at[me, :, cols], gx_s.at[n], gx_r.at[n], partner)
         )
 
+    send_gradient(0)
     for n in range(CHUNKS):
         cols = pl.ds(n * wide, wide)
         to_sibling.append(
@@ -118,8 +119,6 @@
     values = project(acts_pair[x])
     for q in range(4):
         partial[q, x] = values[:, q * quarter:(q + 1) * quarter]
-    acts_copy.wait_send()
-    send_gradient(0)
     acts_copy.wait_recv()
     values = project(acts_pair[ox])
     for q in range(4):
@@ -131,11 +130,11 @@
         coord_copies.append(
             send(partial.at[q], partial_in.at[k], coords_s.at[k], coords_r.at[k], to_dev)
         )
-    send_gradient(1)
+    for n in range(1, CHUNKS):
+        send_gradient(n)
     loads[2].wait()
     for copy in coord_copies:
         copy.wait_recv()
-    send_gradient(2)
     coords[core] = (partial[me] + partial_in[0]).astype(BF16)
     coords[oc] = (partial_in[1] + partial_in[2]).astype(BF16)
 
@@ -165,8 +164,6 @@
     for n in range(CHUNKS):
         cols = pl.ds(n * wide, wide)
         to_partner[n].wait_recv()
-        if n + 3 < CHUNKS:
-            send_gradient(n + 3)
         theirs = core * 2 + ox
         forward.append(
             send(grads.at[theirs, :, cols], grads.at[theirs, :, cols], gf_s.at[n], gf_r.at[n], sibling)
@@ -286,7 +283,7 @@
             copies[kind, j].wait_recv()
     store = pltpu.make_async_copy(gathered, gathered_hbm, out_sem)
     store.start()
-    pending += [back] + to_partner + to_sibling + coord_copies + forward
+    pending += [acts_copy, back] + to_partner + to_sibling + coord_copies + forward
     pending += over_y + scatter + list(copies.values())
     for copy in pending:
         copy.wait_send()

time: 72.6 us -> 72.5 us (level)
  no operation moved by 1% of the time
where the time goes in v6:
time: 72.5 us; the launch traced here: 72.3 us
  Pallas kernels  71.7 us (99%)
    pallas_call x1, Pallas kernels, on_device_kernel(): pl.pallas_call(step_kernel, out_shape=(jax.ShapeDtypeStruct((tokens, d_in...  65.5 us
    pallas_call x1, Pallas kernels, on_device_kernel(): pl.pallas_call(update_kernel, grid=(d_out // wide,), out_shape=[jax.Shape...  6.22 us

profile of v6, /device:TPU:1, one launch (start us, length us, event | category | flops | bytes accessed | tf_op | source)
XLA Modules:
  0.0 72.3 jit_solution(13304345111187849421)
XLA Ops:
  0.6 65.5 %galore_step.1 = (bf16[128,2048]{1,0:T(8,128)(2,1)}, f32[16,2048]{1,0:T(8,128)}, f32[16,2048]{1,0:T(8,128)}, bf16[8,4,16,2048]{3,2,1,0:T(8,128)(2,1)}) custom-call(bf16[128,2048]{1,0:T(8,128)(2,1)} %acts_ref.1, bf16[128,2048]{1,0:T(8,128)(2,1)} %grad_ref.1, bf16[1024,2048]{1,0:T(8,128)(2,1)} %weight_hbm.1, bf16[1024,512]{1,0:T(8,128)(2,1)} %basis_ref.1, ...), custom_call_target="tpu_custom_call" | custom-call | tf_op jit(solution)/shard_map/galore_step/pallas_call | solution.py:312
  66.1 6.2 %back_projection.1 = (bf16[128,2048]{1,0:T(8,128)(2,1)}, f32[16,2048]{1,0:T(8,128)}, f32[16,2048]{1,0:T(8,128)}, bf16[1024,2048]{1,0:T(8,128)(2,1)}) custom-call(bf16[1024,512]{1,0:T(8,128)(2,1)} %basis_ref.1, bf16[512,2048]{1,0:T(8,128)(2,1)} %bitcast.1, bf16[128,2048]{1,0:T(8,128)(2,1)} %get-tuple-element.9.refs_0_, f32[16,2048]{1,0:T(8,128)} %get-tuple-element.10.refs_1_, ...), custom_call_target="tpu_custom_call" | custom-call | tf_op jit(solution)/shard_map/back_projection/pallas_call | solution.py:363

commit v7 on v3

--- a/solution.py
+++ b/solution.py
@@ -17,7 +17,7 @@
 
 PLANES = 8
 DEPTH = PLANES // 2
-CHUNKS = 4
+CHUNKS = 2
 
 
 def clipped_adam(projected, total, first_moment, second_moment, entries):

time: 71.6 us -> 72.2 us (level)
  no operation moved by 1% of the time
where the time goes in v7:
time: 72.2 us; the launch traced here: 72 us
  Pallas kernels  71.3 us (99%)
    pallas_call x1, Pallas kernels, on_device_kernel(): pl.pallas_call(step_kernel, out_shape=(jax.ShapeDtypeStruct((tokens, d_in...  65.1 us
    pallas_call x1, Pallas kernels, on_device_kernel(): pl.pallas_call(update_kernel, grid=(d_out // wide,), out_shape=[jax.Shape...  6.22 us

profile of v7, /device:TPU:1, one launch (start us, length us, event | category | flops | bytes accessed | tf_op | source)
XLA Modules:
  0.0 72.0 jit_solution(9596548994975440195)
XLA Ops:
  0.6 65.1 %galore_step.1 = (bf16[128,2048]{1,0:T(8,128)(2,1)}, f32[16,2048]{1,0:T(8,128)}, f32[16,2048]{1,0:T(8,128)}, bf16[8,4,16,2048]{3,2,1,0:T(8,128)(2,1)}) custom-call(bf16[128,2048]{1,0:T(8,128)(2,1)} %acts_ref.1, bf16[128,2048]{1,0:T(8,128)(2,1)} %grad_ref.1, bf16[1024,2048]{1,0:T(8,128)(2,1)} %weight_hbm.1, bf16[1024,512]{1,0:T(8,128)(2,1)} %basis_ref.1, ...), custom_call_target="tpu_custom_call" | custom-call | tf_op jit(solution)/shard_map/galore_step/pallas_call | solution.py:295
  65.7 6.2 %back_projection.1 = (bf16[128,2048]{1,0:T(8,128)(2,1)}, f32[16,2048]{1,0:T(8,128)}, f32[16,2048]{1,0:T(8,128)}, bf16[1024,2048]{1,0:T(8,128)(2,1)}) custom-call(bf16[1024,512]{1,0:T(8,128)(2,1)} %basis_ref.1, bf16[512,2048]{1,0:T(8,128)(2,1)} %bitcast.1, bf16[128,2048]{1,0:T(8,128)(2,1)} %get-tuple-element.9.refs_0_, f32[16,2048]{1,0:T(8,128)} %get-tuple-element.10.refs_1_, ...), custom_call_target="tpu_custom_call" | custom-call | tf_op jit(solution)/shard_map/back_projection/pallas_call | solution.py:342
